TPU v7x, 32 devices: a whole 2x2x4 slice. The times are simulated.
32 devices in a mesh: req: 8 (over y, x, core), blk: 4 (over z).
Axes of the slice: x: 2, y: 2, z: 4, core: 2. Of those that a mesh axis runs over, the one named last changes fastest.
Arguments:
- x_img: bfloat16 [8, 1024, 1536], P('req', 'blk'), may hold values from -0.3 to 0.3
- x_txt: bfloat16 [8, 154, 1536], P('req'), may hold values from -6 to 6
- modulation: float32 [8, 7, 1536], P('req'), may hold values from -8 to 8
- w_img: bfloat16 [1536, 2304], P(None, 'req'), may hold values from -0.375 to 0.375
- w_txt: bfloat16 [1536, 1536], P(None, 'req'), may hold values from -0.15625 to 0.15625
- w_out: bfloat16 [768, 1536], P('req'), may hold values from -0.21875 to 0.21875
- w_final: bfloat16 [1536, 64], replicated, may hold values from -0.15625 to 0.15625
- lengths: int32 [8], P('req'), may hold values from 16 to 154, as said below
- block_mask: int32 [8, 4, 4], P('req', 'blk'), may hold values from 0 to 1, as said below
- timestep: int32 [8], P('req'), may hold values from 0 to 27
- latent: float32 [8, 16, 32, 128], P('req', None, 'blk'), may hold values from -6 to 6
- conv_w: bfloat16 [512, 144], replicated, may hold values from -0.5 to 0.5
Outputs:
- velocity: float32 [8, 16, 32, 128], P('req', None, 'blk')
- latent_next: float32 [8, 16, 32, 128], P('req', None, 'blk')
- features: bfloat16 [8, 512, 32, 128], P('req', None, 'blk')
Inputs may be any that keep to these rules, and one draw needn't show every extreme that they name: Text keys from position lengths[r] on are padding; some request uses all 154 text tokens. Every tile may attend to its own keys: block_mask[r, t, t] = 1.
All inputs are finite; a program needn't handle non-finite values.
Results may differ from a plain program's by a relative error of at most 0.0063.
Values may be sent and summed in bfloat16 or wider, within the bound.
A program may use at most 192 MiB of HBM per device.

v0:
```python
import jax
import jax.numpy as jnp
from jax import lax
from jax.sharding import PartitionSpec as P

HD = 64
GRIDW = 64
PATCH = 2
LATC = 16
NSTEPS = 28


NORM_EPS = 1e-06
SHIFT_FACTOR = 3.0
LATENT_SCALE = 1.5305
LATENT_SHIFT = 0.0609
NEG_LARGE = -1e30
SCORE_SCALE = 0.125


def with_halo(block, sides, width):
    for axis, dim in sides:
        count = lax.axis_size(axis)
        forward = [(i, i + 1) for i in range(count - 1)]
        backward = [(target, source) for source, target in forward]
        low = lax.ppermute(
            lax.slice_in_dim(block, block.shape[dim] - width, None, axis=dim), axis, forward
        )
        high = lax.ppermute(lax.slice_in_dim(block, 0, width, axis=dim), axis, backward)
        block = jnp.concatenate([low, block, high], axis=dim)
    return block


def layer_norm(values):
    values = values.astype(jnp.float32)
    center = values - jnp.mean(values, axis=-1, keepdims=True)
    spread = jnp.mean(center * center, axis=-1, keepdims=True)
    return center * lax.rsqrt(spread + NORM_EPS)


def modulate(values, shift_row, scale_row):
    return layer_norm(values) * (1.0 + scale_row) + shift_row


def sigma_of(step_index, step_count):
    fraction = 1.0 - step_index.astype(jnp.float32) / step_count
    return SHIFT_FACTOR * fraction / (1.0 + (SHIFT_FACTOR - 1.0) * fraction)


def unpatchify(token_out, grid_width, patch_size, channels):
    patch_rows = token_out.shape[0] // grid_width
    shaped = token_out.reshape(patch_rows, grid_width, patch_size, patch_size, channels)
    shaped = jnp.transpose(shaped, (4, 0, 2, 1, 3))
    return shaped.reshape(channels, patch_rows * patch_size, grid_width * patch_size)


def convolve(padded, conv_w):
    row_count = padded.shape[1] - 2
    col_count = padded.shape[2] - 2
    tap_list = [
        padded[:, tap_row : tap_row + row_count, tap_col : tap_col + col_count]
        for tap_row in range(3)
        for tap_col in range(3)
    ]
    stacked = jnp.stack(tap_list, axis=1).reshape(padded.shape[0] * 9, row_count * col_count)
    convolved = jnp.dot(conv_w, stacked, preferred_element_type=jnp.float32)
    return convolved.reshape(conv_w.shape[0], row_count, col_count)


def text_state(queries, keys_txt, vals_txt, length):
    text_allowed = (jnp.arange(keys_txt.shape[0], dtype=jnp.int32) < length)[None, None, :]
    text_scores = (
        jnp.einsum("qhd,khd->qhk", queries, keys_txt, preferred_element_type=jnp.float32)
        * SCORE_SCALE
    )
    text_scores = jnp.where(text_allowed, text_scores, NEG_LARGE)
    text_max = jnp.max(text_scores, axis=2)
    text_weights = jnp.where(text_allowed, jnp.exp(text_scores - text_max[:, :, None]), 0.0)
    text_acc = jnp.einsum(
        "qhk,khd->qhd",
        text_weights.astype(jnp.bfloat16),
        vals_txt,
        preferred_element_type=jnp.float32,
    )
    return (text_max, jnp.sum(text_weights, axis=2), text_acc)


def absorb_block(previous, queries, head_keys, head_vals, allowed):
    old_max, old_sum, old_acc = previous
    scores = (
        jnp.einsum("qhd,khd->qhk", queries, head_keys, preferred_element_type=jnp.float32)
        * SCORE_SCALE
    )
    scores = jnp.where(allowed, scores, NEG_LARGE)
    new_max = jnp.maximum(old_max, jnp.max(scores, axis=2))
    weights = jnp.where(allowed, jnp.exp(scores - new_max[:, :, None]), 0.0)
    factor = jnp.exp(old_max - new_max)
    summed = jnp.einsum(
        "qhk,khd->qhd", weights.astype(jnp.bfloat16), head_vals, preferred_element_type=jnp.float32
    )
    return (
        new_max,
        old_sum * factor + jnp.sum(weights, axis=2),
        old_acc * factor[:, :, None] + summed,
    )


def absorb_maybe(previous, queries, head_keys, head_vals, allowed):
    return absorb_block(previous, queries, head_keys, head_vals, allowed)


def on_device(
    x_img,
    x_txt,
    modulation,
    w_img,
    w_txt,
    w_out,
    w_final,
    lengths,
    block_mask,
    timestep,
    latent,
    conv_w,
):
    tokens = x_img[0]
    factors = modulation[0]
    tok_rows = tokens.shape[0]
    head_cols = w_out.shape[0] * lax.axis_size("req")
    head_count = head_cols // HD
    h_img = modulate(tokens, factors[0], factors[1]).astype(jnp.bfloat16)
    h_txt = modulate(x_txt[0], factors[3], factors[4]).astype(jnp.bfloat16)
    qkv = jnp.dot(
        h_img, lax.all_gather(w_img, "req", axis=1, tiled=True), preferred_element_type=jnp.float32
    ).astype(jnp.bfloat16)
    kv_txt = jnp.dot(
        h_txt, lax.all_gather(w_txt, "req", axis=1, tiled=True), preferred_element_type=jnp.float32
    ).astype(jnp.bfloat16)
    keys_txt = kv_txt[:, :head_cols].reshape(-1, head_count, HD)
    vals_txt = kv_txt[:, head_cols:].reshape(-1, head_count, HD)
    length = lengths[0]
    queries = qkv[:, :head_cols].reshape(tok_rows, head_count, HD)
    keys_img = qkv[:, head_cols : 2 * head_cols]
    vals_img = qkv[:, 2 * head_cols :]
    mask_row = block_mask[0, 0]
    tile_count = mask_row.shape[0]
    start_state = text_state(queries, keys_txt, vals_txt, length)
    piece_keys = lax.all_gather(keys_img, "blk", axis=0, tiled=True)
    piece_vals = lax.all_gather(vals_img, "blk", axis=0, tiled=True)
    piece_len = piece_keys.shape[0]
    key_tile = jnp.arange(piece_len, dtype=jnp.int32) // tok_rows
    tile_hit = key_tile[:, None] == jnp.arange(tile_count, dtype=jnp.int32)[None, :]
    allowed = jnp.sum(jnp.where(tile_hit, mask_row[None, :], 0), axis=1) == 1
    head_keys = piece_keys.reshape(piece_len, head_count, HD)
    head_vals = piece_vals.reshape(piece_len, head_count, HD)
    run_max, run_sum, run_acc = absorb_maybe(
        start_state, queries, head_keys, head_vals, allowed[None, None, :]
    )
    attended = (run_acc / run_sum[:, :, None]).reshape(tok_rows, head_cols).astype(jnp.bfloat16)
    projected = jnp.dot(
        attended,
        lax.all_gather(w_out, "req", axis=0, tiled=True),
        preferred_element_type=jnp.float32,
    )
    residual = tokens.astype(jnp.float32) + factors[2] * projected
    final_in = modulate(residual, factors[5], factors[6]).astype(jnp.bfloat16)
    token_out = jnp.dot(final_in, w_final, preferred_element_type=jnp.float32)
    velocity = unpatchify(token_out, GRIDW, PATCH, LATC)[None]
    step_index = timestep[0]
    sigma_step = sigma_of(step_index + 1, NSTEPS) - sigma_of(step_index, NSTEPS)
    latent_next = latent + sigma_step * velocity
    decoded = (latent_next / LATENT_SCALE + LATENT_SHIFT).astype(jnp.bfloat16)
    padded = with_halo(decoded, (("blk", 2),), 1)
    padded = jnp.pad(padded[0], ((0, 0), (0, 0), (1, 1)))
    features = convolve(padded, conv_w).astype(jnp.bfloat16)[None]
    return (velocity, latent_next, features)


def solution(mesh):
    return jax.shard_map(
        on_device,
        mesh=mesh,
        in_specs=(
            P("req", "blk", None),
            P("req", None, None),
            P("req", None, None),
            P(None, "req"),
            P(None, "req"),
            P("req", None),
            P(),
            P("req"),
            P("req", "blk", None),
            P("req"),
            P("req", None, "blk", None),
            P(),
        ),
        out_specs=(
            P("req", None, "blk", None),
            P("req", None, "blk", None),
            P("req", None, "blk", None),
        ),
        check_vma=False,
    )
```

profile of v0, /device:TPU:16, one launch (start us, length us, event | category | flops | bytes accessed | tf_op | source)
XLA Modules:
  0.0 228.5 jit_solution(16971153236048344387)
XLA Ops:
  7.2 0.7 all-gather.8.cloned.1.call-update
  8.0 0.7 all-gather.6.cloned.1.call-update
  8.7 0.9 add_reduce_fusion
  9.6 0.2 convert_reduce_fusion
  9.8 0.3 fusion.14
  10.2 49.7 %all-gather.8.cloned.1.call-done = bf16[1536,2304]{0,1:T(8,128)(2,1)} async-done(((bf16[1536,288]{0,1:T(8,128)(2,1)}), bf16[1536,2304]{0,1:T(8,128)(2,1)}) %all-gather.8.cloned.1.call-update) | async-done | bytes 7077904 | tf_op jit(solution)/shard_map/all_gather | solution.py:134
  59.9 5.2 %convolution_convert_fusion = bf16[256,2304]{1,0:T(8,128)(2,1)S(1)} fusion(bf16[1536,2304]{0,1:T(8,128)(2,1)} %all-gather.8.cloned.1.call-done, bf16[1,256,1536]{2,1,0:T(8,128)(2,1)S(1)} %copy-done.2, f32[1536]{0:T(1024)S(1)} %get-tuple-element.16, f32[1536]{0:T(1024)S(1)} %get-tuple-element.17, f32[256]{0:T(256)S(1)} %add_rsqrt_fusion.1, ...), kind=kOutput, calls=%fused_computation.10 | convolution fusion | flops 1814888448 | bytes 9058304 | tf_op jit(solution)/shard_map/dot_general | solution.py:133
  65.1 1.0 fusion.69
  66.1 0.5 all-gather.12.cloned.1.call-update
  66.7 0.5 all-gather.14.cloned.1.call-update
  67.9 0.1 convert_reduce_fusion.1
  68.1 0.3 fusion.30
  69.0 0.1 select_reduce_fusion
  69.2 1.0 copy.66
  70.3 30.4 %all-gather.6.cloned.1.call-done = bf16[1536,1536]{0,1:T(8,128)(2,1)} async-done(((bf16[1536,192]{0,1:T(8,128)(2,1)}), bf16[1536,1536]{0,1:T(8,128)(2,1)}) %all-gather.6.cloned.1.call-update) | async-done | bytes 4718608 | tf_op jit(solution)/shard_map/all_gather | solution.py:137
  100.7 4.0 %convolution_convert_fusion.1 = bf16[154,1536]{1,0:T(8,128)(2,1)S(1)} fusion(bf16[1536,1536]{0,1:T(8,128)(2,1)} %all-gather.6.cloned.1.call-done, bf16[1,154,1536]{2,1,0:T(8,128)(2,1)S(1)} %copy-done.4, f32[1536]{0:T(1024)S(1)} %get-tuple-element.18, f32[1536]{0:T(1024)S(1)} %get-tuple-element.19, f32[154]{0:T(256)S(1)} %add_rsqrt_fusion.2, ...), kind=kOutput, calls=%fused_computation.13 | convolution fusion | flops 728318976 | bytes 5678288 | tf_op jit(solution)/shard_map/dot_general | solution.py:136
  104.8 0.9 copy.60
  105.7 0.9 copy.59
  106.6 0.2 copy.61
  106.8 1.6 bitcast_reduce_fusion.1
  108.4 0.6 fusion.18
  108.9 29.3 %all-gather.10.cloned.1.call-done = bf16[1024,768]{1,0:T(8,128)(2,1)} async-done(((bf16[256,768]{1,0:T(8,128)(2,1)}), bf16[1024,768]{1,0:T(8,128)(2,1)}) %all-gather.10.cloned.1.call-update) | async-done | bytes 1572880 | tf_op jit(solution)/shard_map/all_gather | solution.py:148
  138.3 2.6 %copy.62 = bf16[1024,768]{0,1:T(8,128)(2,1)} copy(bf16[1024,768]{1,0:T(8,128)(2,1)} %all-gather.10.cloned.1.call-done) | data formatting | bytes 3145728 | tf_op jit(solution)/shard_map/all_gather | solution.py:148
  140.9 8.8 %bitcast_reduce_fusion = (f32[256,12]{0,1:T(8,128)S(1)}, f32[12,1024,256]{2,1,0:T(8,128)}) fusion(pred[1024]{0:T(1024)(128)(4,1)S(1)} %broadcast_compare_fusion, bf16[1024,12,64]{0,2,1:T(8,128)(2,1)} %bitcast.129, bf16[256,12,64]{0,2,1:T(8,128)(2,1)S(1)} %bitcast.134), kind=kOutput, calls=%fused_computation.1 | convolution fusion | flops 412087296 | bytes 14562304 | tf_op jit(solution)/shard_map/qhd,khd->qhk/dot_general | solution.py:91
  149.7 26.0 %all-gather.12.cloned.1.call-done = bf16[1024,768]{1,0:T(8,128)(2,1)} async-done(((bf16[256,768]{1,0:T(8,128)(2,1)}), bf16[1024,768]{1,0:T(8,128)(2,1)}) %all-gather.12.cloned.1.call-update) | async-done | bytes 1572880 | tf_op jit(solution)/shard_map/all_gather | solution.py:149
  175.7 2.6 %copy.63 = bf16[1024,768]{0,1:T(8,128)(2,1)} copy(bf16[1024,768]{1,0:T(8,128)(2,1)} %all-gather.12.cloned.1.call-done) | data formatting | bytes 3145728 | tf_op jit(solution)/shard_map/all_gather | solution.py:149
  178.3 7.0 %fusion.2 = f32[256,12]{0,1:T(8,128)S(1)} fusion(f32[12,1024,256]{2,1,0:T(8,128)} %get-tuple-element.45, f32[256,12]{0,1:T(8,128)S(1)} %max.13, pred[1024]{0:T(1024)(128)(4,1)S(1)} %broadcast_compare_fusion), kind=kLoop, calls=%fused_computation.5 | loop fusion | flops 15725568 | bytes 12608512 | tf_op jit(solution)/shard_map/reduce_sum | solution.py:103
  185.3 1.5 copy-done.1
  186.8 4.3 %fusion.20 = f32[256,12,64]{0,2,1:T(8,128)S(1)} fusion(bf16[1024,12,64]{0,2,1:T(8,128)(2,1)} %bitcast.135, f32[12,1024,256]{2,1,0:T(8,128)S(1)} %copy-done.1, f32[256,12]{0,1:T(8,128)S(1)} %max.13, pred[1024]{0:T(1024)(128)(4,1)S(1)} %broadcast_compare_fusion), kind=kOutput, calls=%fused_computation.33 | convolution fusion | flops 418381824 | bytes 14955520 | tf_op jit(solution)/shard_map/qhk,khd->qhd/dot_general | solution.py:98
  191.1 0.7 fusion.26
  191.8 14.7 %all-gather.14.cloned.1.call-done = bf16[768,1536]{1,0:T(8,128)(2,1)} async-done(((bf16[96,1536]{1,0:T(8,128)(2,1)}), bf16[768,1536]{1,0:T(8,128)(2,1)}) %all-gather.14.cloned.1.call-update) | async-done | bytes 2359312 | tf_op jit(solution)/shard_map/all_gather | solution.py:162
  206.5 2.5 %fusion.72 = (f32[256]{0:T(256)S(1)}, f32[256,1536]{1,0:T(8,128)S(1)}) fusion(bf16[256,768]{0,1:T(8,128)(2,1)S(1)} %bitcast.137, bf16[768,1536]{1,0:T(8,128)(2,1)} %all-gather.14.cloned.1.call-done, f32[1536]{0:T(1024)S(1)} %get-tuple-element.20, bf16[1,256,1536]{2,1,0:T(8,128)(2,1)S(1)} %copy-done.2), kind=kOutput, calls=%fused_computation.127 | convolution fusion | flops 605552384 | bytes 5118976 | tf_op jit(solution)/shard_map/dot_general | solution.py:160
  209.0 0.3 multiply_reduce_fusion
  209.3 0.5 fusion.46
  209.8 0.1 reshape.190
  209.9 0.3 copy.65
  210.2 0.1 add_convert_fusion.2
  210.4 3.4 %collective-permute-start = (bf16[1,16,1,128]{1,3,2,0:T(8,128)(2,1)S(1)}, bf16[1,16,1,128]{1,3,2,0:T(8,128)(2,1)S(1)}, u32[]{:S(2)}, u32[]{:S(2)}) collective-permute-start(bf16[1,16,1,128]{1,3,2,0:T(8,128)(2,1)S(1)} %get-tuple-element.31), channel_id=1, source_target_pairs={{0,1},{1,2},{2,3},{4,5},{5,6},{6,7},{8,9},{9,10},{10,11},{12,13},{... | collective-permute-start | bytes 12296 | tf_op jit(solution)/shard_map/ppermute | solution.py:26
  213.8 2.4 %collective-permute-start.1 = (bf16[1,16,1,128]{1,3,2,0:T(8,128)(2,1)S(1)}, bf16[1,16,1,128]{1,3,2,0:T(8,128)(2,1)S(1)}, u32[]{:S(2)}, u32[]{:S(2)}) collective-permute-start(bf16[1,16,1,128]{1,3,2,0:T(8,128)(2,1)S(1)} %get-tuple-element.32), channel_id=1, source_target_pairs={{1,0},{2,1},{3,2},{5,4},{6,5},{7,6},{9,8},{10,9},{11,10},{13,12},{... | collective-permute-start | bytes 12296 | tf_op jit(solution)/shard_map/ppermute | solution.py:29
  216.2 0.1 copy.68
  216.3 0.8 copy.79
  217.1 0.8 copy.80
  217.9 0.1 copy.67
  218.0 1.6 collective-permute-done.1
  219.6 0.1 copy.69
  219.7 0.1 fusion.59
  220.0 0.5 convolution_convert_fusion.2
  220.5 1.5 copy.81
  (47 shorter events, 0.6 us)
Async XLA Ops:
  7.2 202.2 %copy-start = (bf16[1536,64]{0,1:T(8,128)(2,1)S(1)}, bf16[1536,64]{0,1:T(8,128)(2,1)}, u32[]{:S(2)}) copy-start(bf16[1536,64]{0,1:T(8,128)(2,1)} %param.18) | copy-start | bytes 589828
  7.2 2.5 %copy-start.2 = (bf16[1,256,1536]{2,1,0:T(8,128)(2,1)S(1)}, bf16[1,256,1536]{2,1,0:T(8,128)(2,1)}, u32[]{:S(2)}) copy-start(bf16[1,256,1536]{2,1,0:T(8,128)(2,1)} %param.12) | copy-start | bytes 2359300
  7.2 52.7 %all-gather.8.cloned.1.call-start = ((), (), s32[]{:S(2)}) async-start(), calls=%async_computation.1 | async-start | bytes 7962624 | tf_op jit(solution)/shard_map/all_gather | solution.py:134
  7.9 92.8 %all-gather.6.cloned.1.call-start = ((), (), s32[]{:S(2)}) async-start(), calls=%async_computation | async-start | bytes 5308416 | tf_op jit(solution)/shard_map/all_gather | solution.py:137
  8.7 129.6 %all-gather.10.cloned.1.call-start = ((), (), s32[]{:S(2)}) async-start(), calls=%async_computation.2 | async-start | bytes 1966080 | tf_op jit(solution)/shard_map/all_gather | solution.py:148
  65.0 2.9 %copy-start.4 = (bf16[1,154,1536]{2,1,0:T(8,128)(2,1)S(1)}, bf16[1,154,1536]{2,1,0:T(8,128)(2,1)}, u32[]{:S(2)}) copy-start(bf16[1,154,1536]{2,1,0:T(8,128)(2,1)} %param.13) | copy-start | bytes 1419268
  65.0 4.0 %copy-start.8 = (s32[1,1,4]{2,1,0:T(1,128)S(1)}, s32[1,1,4]{2,1,0:T(1,128)}, u32[]{:S(2)}) copy-start(s32[1,1,4]{2,1,0:T(1,128)} %param.20) | copy-start | bytes 52
  65.1 4.1 %copy-start.7 = (f32[1,16,8,128]{3,2,1,0:T(8,128)S(1)}, f32[1,16,8,128]{3,2,1,0:T(8,128)}, u32[]{:S(2)}) copy-start(f32[1,16,8,128]{3,2,1,0:T(8,128)} %param.22) | copy-start | bytes 196612
  66.1 109.6 %all-gather.12.cloned.1.call-start = ((), (), s32[]{:S(2)}) async-start(), calls=%async_computation.3 | async-start | bytes 1966080 | tf_op jit(solution)/shard_map/all_gather | solution.py:149
  66.6 139.8 %all-gather.14.cloned.1.call-start = ((), (), s32[]{:S(2)}) async-start(), calls=%async_computation.4 | async-start | bytes 2654208 | tf_op jit(solution)/shard_map/all_gather | solution.py:162
  178.3 8.5 %copy-start.1 = (f32[12,1024,256]{2,1,0:T(8,128)S(1)}, f32[12,1024,256]{2,1,0:T(8,128)}, u32[]{:S(2)}) copy-start(f32[12,1024,256]{2,1,0:T(8,128)} %get-tuple-element.45) | copy-start | bytes 37748740
  186.8 4.3 %copy-start.5 = (bf16[154,768]{0,1:T(8,128)(2,1)S(1)}, bf16[154,768]{0,1:T(8,128)(2,1)}, u32[]{:S(2)}) copy-start(bf16[154,768]{0,1:T(8,128)(2,1)} %copy.59) | copy-start | bytes 709636
  209.0 1.2 copy-start.3
  210.2 9.8 %copy-start.6 = (bf16[512,144]{0,1:T(8,128)(2,1)S(1)}, bf16[512,144]{0,1:T(8,128)(2,1)}, u32[]{:S(2)}) copy-start(bf16[512,144]{0,1:T(8,128)(2,1)} %param.23) | copy-start | bytes 442372
  210.4 7.6 %collective-permute-start = (bf16[1,16,1,128]{1,3,2,0:T(8,128)(2,1)S(1)}, bf16[1,16,1,128]{1,3,2,0:T(8,128)(2,1)S(1)}, u32[]{:S(2)}, u32[]{:S(2)}) collective-permute-start(bf16[1,16,1,128]{1,3,2,0:T(8,128)(2,1)S(1)} %get-tuple-element.31), channel_id=1, source_target_pairs={{0,1},{1,2},{2,3},{4,5},{5,6},{6,7},{8,9},{9,10},{10,11},{12,13},{... | collective-permute-start | bytes 12296 | tf_op jit(solution)/shard_map/ppermute | solution.py:26
  213.8 5.8 %collective-permute-start.1 = (bf16[1,16,1,128]{1,3,2,0:T(8,128)(2,1)S(1)}, bf16[1,16,1,128]{1,3,2,0:T(8,128)(2,1)S(1)}, u32[]{:S(2)}, u32[]{:S(2)}) collective-permute-start(bf16[1,16,1,128]{1,3,2,0:T(8,128)(2,1)S(1)} %get-tuple-element.32), channel_id=1, source_target_pairs={{1,0},{2,1},{3,2},{5,4},{6,5},{7,6},{9,8},{10,9},{11,10},{13,12},{... | collective-permute-start | bytes 12296 | tf_op jit(solution)/shard_map/ppermute | solution.py:29
Sparse Core Ops, SparseCore 0:
  9.9 49.9 all-gather.7
  61.7 38.9 all-gather.5
  102.3 35.9 all-gather.9
  139.7 35.9 all-gather.11
  177.4 28.9 all-gather.13
where the time goes:
time: 231 us; the launch traced here: 228 us
  waiting for transfers between devices  154 us (67%)
  matrix products  28 us (12%)
  between operations  15.5 us (7%)
  local copies, waits for them, and re-layouts  14.7 us (6%)
  other arithmetic  10 us (4%)
  starting transfers between devices  6.04 us (3%)
    all_gather x1, waiting for transfers between devices, on_device(): lax.all_gather(w_img, 'req', axis=1, tiled=True)  49.7 us
    all_gather x1, waiting for transfers between devices, on_device(): lax.all_gather(w_txt, 'req', axis=1, tiled=True)  30.4 us
    all_gather x1, waiting for transfers between devices, on_device(): piece_keys = lax.all_gather(keys_img, 'blk', axis=0, tiled=True)  29.3 us
    all_gather x1, waiting for transfers between devices, on_device(): piece_vals = lax.all_gather(vals_img, 'blk', axis=0, tiled=True)  26 us
    all_gather x1, waiting for transfers between devices, on_device(): lax.all_gather(w_out, 'req', axis=0, tiled=True)  14.7 us
    dot_general x1, matrix products, absorb_block(): jnp.einsum('qhd,khd->qhk', queries, head_keys, preferred_element_type=jnp...  8.82 us
    reduce_sum x1, other arithmetic, absorb_block(): jnp.sum(weights, axis=2)  7.02 us
    unnamed x30, local copies, waits for them, and re-layouts  5.76 us
  transfers between devices with their start and end apart: 7, of which 6 were waited for; matrix products, arithmetic and copies ran while one was open for 20% of the time, Pallas kernels for 0%

commit v1 on v0

--- a/solution.py
+++ b/solution.py
@@ -1,6 +1,8 @@
 import jax
 import jax.numpy as jnp
 from jax import lax
+from jax.experimental import pallas as pl
+from jax.experimental.pallas import tpu as pltpu
 from jax.sharding import PartitionSpec as P
 
 HD = 64
@@ -176,9 +178,383 @@
     return (velocity, latent_next, features)
 
 
+MESH = pl.DeviceIdType.MESH
+NTILE = 4
+NREQ = 8
+CHUNK = 96
+TXT_PAD = 256
+F32 = jnp.float32
+BF16 = jnp.bfloat16
+
+
+def nt_dot(a, b):
+    return lax.dot_general(a, b, (((1,), (1,)), ((), ())), preferred_element_type=F32)
+
+
+def flip(r, bit):
+    return r + bit - 2 * bit * ((r // bit) % 2)
+
+
+def normed(v):
+    v = v.astype(F32)
+    c = v - jnp.mean(v, axis=-1, keepdims=True)
+    return c * lax.rsqrt(jnp.mean(c * c, axis=-1, keepdims=True) + NORM_EPS)
+
+
+def kernel(
+    x_ref, xt_ref, mod_ref, wi_ref, wt_ref, wo_ref, wf_ref, bias_ref, ss_ref, lat_ref,
+    vel_ref, next_ref, stk_ref,
+    H, HT, WI, WT, WO, Q, K, V, BIAS, A, AT, FIN, DEC,
+    z_send, h_recv, b_send, b_recv, wi_send, wi_recv, wt_send, wt_recv,
+    wo_send, wo_recv, a_send, a_recv, d_send, d_recv, l_sem,
+):
+    r = lax.axis_index("req")
+    z = lax.axis_index("blk")
+    rows = x_ref.shape[0]
+    tokens = rows * NTILE
+    group = WI.shape[0] // 3
+    sib = flip(r, 1)
+    nx = flip(r, 2)
+    ny = flip(r, 4)
+    nd = flip(nx, 4)
+
+    def rcopy(src, dst, ss, rs, **dev):
+        return pltpu.make_async_remote_copy(
+            src_ref=src, dst_ref=dst, send_sem=ss, recv_sem=rs, device_id=dev, device_id_type=MESH
+        )
+
+    barrier = pltpu.get_barrier_semaphore()
+    for step in range(1, NREQ):
+        pl.semaphore_signal(
+            barrier, inc=1, device_id={"req": lax.rem(r + step, NREQ)}, device_id_type=MESH
+        )
+    for step in range(1, NTILE):
+        pl.semaphore_signal(
+            barrier, inc=1, device_id={"blk": lax.rem(z + step, NTILE)}, device_id_type=MESH
+        )
+    pl.semaphore_wait(barrier, NREQ - 1 + NTILE - 1)
+
+    pieces = []
+    for j in range(6):
+        cid = 8 * (j // 2) + 2 * z + j % 2
+        off = pl.multiple_of((cid % 3) * CHUNK, CHUNK)
+        pieces.append(
+            (wi_ref.at[pl.ds(off, CHUNK)], WI.at[pl.ds(j * CHUNK, CHUNK)], cid // 3, wi_send.at[j], wi_recv.at[j], l_sem.at[j])
+        )
+    for j in range(2):
+        pieces.append(
+            (wt_ref, WT.at[pl.ds(j * group, group)], 4 * j + z, wt_send.at[j], wt_recv.at[j], l_sem.at[6 + j])
+        )
+
+    for src, slot, owner, ss, rs, ls in pieces:
+        @pl.when(owner == r)
+        def _():
+            for n, dev in enumerate((nx, ny, nd, sib)):
+                rcopy(src, slot, ss.at[n], rs, req=dev).start()
+            pltpu.make_async_copy(src, slot, ls).start()
+
+    def norm_rows(i, src, dst, shift, scale):
+        at = pl.ds(pl.multiple_of(i * 32, 32), 32)
+        dst[at, :] = (normed(src[at, :]) * (1.0 + mod_ref[scale : scale + 1, :]) + mod_ref[shift : shift + 1, :]).astype(BF16)
+
+    own = H.at[z]
+    pl.loop(0, rows // 32)(lambda i: norm_rows(i, x_ref, own, 0, 1))
+
+    def up(t):
+        return rcopy(H.at[t], H.at[t], z_send.at[0, t], h_recv.at[t], blk=z + 1)
+
+    def down(t):
+        return rcopy(H.at[t], H.at[t], z_send.at[1, t], h_recv.at[t], blk=z - 1)
+
+    @pl.when(z < NTILE - 1)
+    def _():
+        up(z).start()
+
+    @pl.when(z > 0)
+    def _():
+        down(z).start()
+
+    BIAS[z] = bias_ref[...]
+    for step in range(1, NTILE):
+        rcopy(BIAS.at[z], BIAS.at[z], b_send.at[step], b_recv.at[NTILE - step], blk=lax.rem(z + step, NTILE)).start()
+
+    pl.loop(0, TXT_PAD // 32)(lambda i: norm_rows(i, xt_ref, HT, 3, 4))
+
+    for src, slot, owner, ss, rs, ls in pieces:
+        @pl.when(owner == r)
+        def _():
+            pltpu.make_async_copy(src, slot, ls).wait()
+
+        @pl.when(owner != r)
+        def _():
+            rcopy(src, slot, ss.at[0], rs, req=sib).wait_recv()
+
+        far = jnp.logical_and(owner // 2 != r // 2, owner % 2 == r % 2)
+
+        @pl.when(far)
+        def _():
+            rcopy(slot, slot, ss.at[0], rs, req=sib).start()
+
+    def wo_rows(dev):
+        return WO.at[pl.ds(pl.multiple_of(dev * CHUNK, CHUNK), CHUNK)]
+
+    for n, (k, dev) in enumerate(((2, nx), (4, ny), (6, nd), (1, sib))):
+        rcopy(wo_ref, wo_rows(r), wo_send.at[n], wo_recv.at[k], req=dev).start()
+    pltpu.make_async_copy(wo_ref, wo_rows(r), l_sem.at[8]).start()
+
+    kv = nt_dot(HT[...], WT[...]).astype(BF16)
+    K[tokens:, :] = kv[:, :group]
+    V[tokens:, :] = kv[:, group:]
+
+    def project(t):
+        at = pl.ds(pl.multiple_of(t * rows, rows), rows)
+        qkv = nt_dot(H[t], WI[...]).astype(BF16)
+        Q[at, :] = qkv[:, :group] * jnp.asarray(SCORE_SCALE, BF16)
+        K[at, :] = qkv[:, group : 2 * group]
+        V[at, :] = qkv[:, 2 * group :]
+
+    project(z)
+    for step in range(1, NTILE):
+        low, high = z - step, z + step
+
+        @pl.when(low >= 0)
+        def _():
+            rcopy(H.at[low], H.at[low], z_send.at[0, low], h_recv.at[low], blk=z).wait_recv()
+
+            @pl.when(z < NTILE - 1)
+            def _():
+                up(low).start()
+
+        @pl.when(high < NTILE)
+        def _():
+            rcopy(H.at[high], H.at[high], z_send.at[1, high], h_recv.at[high], blk=z).wait_recv()
+
+            @pl.when(z > 0)
+            def _():
+                down(high).start()
+
+        if step == 1:
+            for n, (k, dev) in enumerate(((2, nx), (4, ny), (6, nd))):
+                rows_of = wo_rows(dev)
+                rcopy(wo_ref, rows_of, wo_send.at[n], wo_recv.at[k], req=sib).wait_recv()
+                rcopy(rows_of, rows_of, wo_send.at[4 + n], wo_recv.at[k + 1], req=sib).start()
+
+        @pl.when(low >= 0)
+        def _():
+            project(low)
+
+        @pl.when(high < NTILE)
+        def _():
+            project(high)
+
+    for step in range(1, NTILE):
+        src = BIAS.at[lax.rem(z + step, NTILE)]
+        rcopy(src, src, b_send.at[step], b_recv.at[step], blk=lax.rem(z + step, NTILE)).wait_recv()
+
+    def attend(t):
+        at = pl.ds(pl.multiple_of(t * rows, rows), rows)
+        bias = BIAS[t][0:1, :]
+        q, k, v = Q[at, :], K[...], V[...]
+        outs = []
+        for h in range(group // HD):
+            cols = slice(h * HD, (h + 1) * HD)
+            s = nt_dot(q[:, cols], k[:, cols]) + bias
+            p = jnp.exp(s - jnp.max(s, axis=1, keepdims=True))
+            total = jnp.sum(p, axis=1, keepdims=True)
+            o = jnp.dot(p.astype(BF16), v[:, cols], preferred_element_type=F32)
+            outs.append(o / total)
+        return jnp.concatenate(outs, axis=1).astype(BF16)
+
+    for step in range(1, NTILE):
+        t = lax.rem(z + step, NTILE)
+        A[step] = attend(t)
+        rcopy(A.at[step], AT.at[z], a_send.at[step], a_recv.at[NTILE - step], blk=t).start()
+    AT[z] = attend(z)
+
+    pltpu.make_async_copy(wo_ref, wo_rows(r), l_sem.at[8]).wait()
+    rcopy(wo_ref, wo_rows(sib), wo_send.at[3], wo_recv.at[1], req=sib).wait_recv()
+    for n, (k, dev) in enumerate(((3, nx), (5, ny), (7, nd))):
+        rcopy(wo_ref, wo_rows(flip(dev, 1)), wo_send.at[4 + n], wo_recv.at[k], req=sib).wait_recv()
+    for step in range(1, NTILE):
+        src = AT.at[lax.rem(z + step, NTILE)]
+        rcopy(src, src, a_send.at[step], a_recv.at[step], blk=lax.rem(z + step, NTILE)).wait_recv()
+
+    def out_rows(i):
+        at = pl.ds(pl.multiple_of(i * 64, 64), 64)
+        proj = jnp.dot(AT[0, at, :], WO[0:group, :], preferred_element_type=F32)
+        for s in range(1, NTILE):
+            proj += jnp.dot(AT[s, at, :], WO[s * group : (s + 1) * group, :], preferred_element_type=F32)
+        res = x_ref[at, :].astype(F32) + mod_ref[2:3, :] * proj
+        FIN[at, :] = (normed(res) * (1.0 + mod_ref[6:7, :]) + mod_ref[5:6, :]).astype(BF16)
+
+    pl.loop(0, rows // 64)(out_rows)
+
+    dup = (
+        lax.broadcasted_iota(jnp.int32, (2 * rows, rows), 0) // 2
+        == lax.broadcasted_iota(jnp.int32, (2 * rows, rows), 1)
+    ).astype(F32).astype(BF16)
+    twice = jnp.dot(dup, FIN[...], preferred_element_type=F32).astype(BF16)
+    tok = jnp.dot(twice, wf_ref[...], preferred_element_type=F32).T
+    even = lax.broadcasted_iota(jnp.int32, (LATC, 2 * rows), 1) % 2 == 0
+    width = PATCH * GRIDW
+    sig = ss_ref[0:1, :]
+    for p in range(PATCH):
+        base = p * 2 * LATC
+        val = jnp.where(even, tok[base : base + LATC], tok[base + LATC : base + 2 * LATC])
+        for a in range(rows // GRIDW):
+            y = PATCH * a + p
+            piece = val[:, a * width : (a + 1) * width]
+            nxt = lat_ref[:, y, :] + sig * piece
+            vel_ref[:, y, :] = piece
+            next_ref[:, y, :] = nxt
+            DEC[y + 1] = (nxt / LATENT_SCALE + LATENT_SHIFT).astype(BF16)
+
+    count = PATCH * rows // GRIDW
+    go_up = rcopy(DEC.at[count], DEC.at[0], d_send.at[0], d_recv.at[0], blk=z + 1)
+    go_down = rcopy(DEC.at[1], DEC.at[count + 1], d_send.at[1], d_recv.at[1], blk=z - 1)
+
+    @pl.when(z < NTILE - 1)
+    def _():
+        go_up.start()
+
+    @pl.when(z > 0)
+    def _():
+        go_down.start()
+
+    @pl.when(z == 0)
+    def _():
+        DEC[0] = jnp.zeros((LATC, width), BF16)
+
+    @pl.when(z == NTILE - 1)
+    def _():
+        DEC[count + 1] = jnp.zeros((LATC, width), BF16)
+
+    for src, slot, owner, ss, rs, ls in pieces:
+        @pl.when(owner == r)
+        def _():
+            for n, dev in enumerate((nx, ny, nd, sib)):
+                rcopy(src, slot, ss.at[n], rs, req=dev).wait_send()
+
+        far = jnp.logical_and(owner // 2 != r // 2, owner % 2 == r % 2)
+
+        @pl.when(far)
+        def _():
+            rcopy(slot, slot, ss.at[0], rs, req=sib).wait_send()
+
+    for n in range(7):
+        rcopy(wo_ref, wo_rows(r), wo_send.at[n], wo_recv.at[1], req=sib).wait_send()
+    for t in range(NTILE):
+        @pl.when(jnp.logical_and(z < NTILE - 1, t <= z))
+        def _():
+            up(t).wait_send()
+
+        @pl.when(jnp.logical_and(z > 0, t >= z))
+        def _():
+            down(t).wait_send()
+    for step in range(1, NTILE):
+        there = lax.rem(z + step, NTILE)
+        rcopy(BIAS.at[z], BIAS.at[z], b_send.at[step], b_recv.at[step], blk=there).wait_send()
+        rcopy(A.at[step], AT.at[z], a_send.at[step], a_recv.at[step], blk=there).wait_send()
+
+    @pl.when(z < NTILE - 1)
+    def _():
+        go_up.wait_send()
+        go_down.wait_recv()
+
+    @pl.when(z > 0)
+    def _():
+        go_down.wait_send()
+        go_up.wait_recv()
+
+    lane = lax.broadcasted_iota(jnp.int32, (LATC, width), 1)
+    for yy in range(count + 2):
+        mid = DEC[yy].astype(F32)
+        shifted = (
+            jnp.where(lane == 0, 0.0, pltpu.roll(mid, 1, 1)),
+            mid,
+            jnp.where(lane == width - 1, 0.0, pltpu.roll(mid, width - 1, 1)),
+        )
+        for a in range(3):
+            y = yy - a
+            if 0 <= y < count:
+                for b in range(3):
+                    at = (3 * a + b) * LATC
+                    stk_ref[at : at + LATC, y * width : (y + 1) * width] = shifted[b].astype(BF16)
+
+
+def split_heads(
+    x_img, x_txt, modulation, w_img, w_txt, w_out, w_final, lengths, block_mask, timestep, latent, conv_w
+):
+    rows, model = x_img.shape[1], x_img.shape[2]
+    group = w_out.shape[0] * NREQ // NTILE
+    tokens = rows * NTILE
+    allowed = jnp.concatenate(
+        [jnp.repeat(block_mask[0, 0] == 1, rows), jnp.arange(TXT_PAD, dtype=jnp.int32) < lengths[0]]
+    )
+    bias = jnp.broadcast_to(jnp.where(allowed, 0.0, NEG_LARGE).astype(F32)[None, :], (8, tokens + TXT_PAD))
+    step_index = timestep[0]
+    sigma_step = sigma_of(step_index + 1, NSTEPS) - sigma_of(step_index, NSTEPS)
+    height, width = latent.shape[2], latent.shape[3]
+    xt = jnp.pad(x_txt[0], ((0, TXT_PAD - x_txt.shape[1]), (0, 0)))
+    vmem = pl.BlockSpec(memory_space=pltpu.VMEM)
+    hbm = pl.BlockSpec(memory_space=pl.ANY)
+    dma = pltpu.SemaphoreType.DMA
+    velocity, latent_next, stacked = pl.pallas_call(
+        kernel,
+        out_shape=(
+            jax.ShapeDtypeStruct((LATC, height, width), F32),
+            jax.ShapeDtypeStruct((LATC, height, width), F32),
+            jax.ShapeDtypeStruct((9 * LATC, height * width), BF16),
+        ),
+        in_specs=[vmem, vmem, vmem, hbm, hbm, hbm, vmem, vmem, vmem, vmem],
+        out_specs=(vmem, vmem, vmem),
+        scratch_shapes=[
+            pltpu.VMEM((NTILE, rows, model), BF16),
+            pltpu.VMEM((TXT_PAD, model), BF16),
+            pltpu.VMEM((3 * group, model), BF16),
+            pltpu.VMEM((2 * group, model), BF16),
+            pltpu.VMEM((NTILE * group, model), BF16),
+            pltpu.VMEM((tokens, group), BF16),
+            pltpu.VMEM((tokens + TXT_PAD, group), BF16),
+            pltpu.VMEM((tokens + TXT_PAD, group), BF16),
+            pltpu.VMEM((NTILE, 8, tokens + TXT_PAD), F32),
+            pltpu.VMEM((NTILE, rows, group), BF16),
+            pltpu.VMEM((NTILE, rows, group), BF16),
+            pltpu.VMEM((rows, model), BF16),
+            pltpu.VMEM((height + 2, LATC, width), BF16),
+            dma((2, NTILE)),
+            dma((NTILE,)),
+            dma((NTILE,)),
+            dma((NTILE,)),
+            dma((6, 4)),
+            dma((6,)),
+            dma((2, 4)),
+            dma((2,)),
+            dma((7,)),
+            dma((8,)),
+            dma((NTILE,)),
+            dma((NTILE,)),
+            dma((2,)),
+            dma((2,)),
+            dma((9,)),
+        ],
+        compiler_params=pltpu.CompilerParams(
+            collective_id=0, has_side_effects=True, vmem_limit_bytes=48 * 1024 * 1024
+        ),
+        name="split_heads",
+    )(
+        x_img[0], xt, modulation[0], w_img.T, w_txt.T, w_out, w_final, bias,
+        jnp.full((8, width), sigma_step, F32), latent[0],
+    )
+    taps = conv_w.reshape(-1, LATC, 9).transpose(0, 2, 1).reshape(-1, 9 * LATC)
+    features = jnp.dot(taps, stacked, preferred_element_type=F32).astype(BF16)
+    return velocity[None], latent_next[None], features.reshape(1, -1, height, width)
+
+
 def solution(mesh):
+    fits = mesh.shape["blk"] == NTILE and mesh.shape["req"] == NREQ
     return jax.shard_map(
-        on_device,
+        split_heads if fits else on_device,
         mesh=mesh,
         in_specs=(
             P("req", "blk", None),

time: 231 us -> 108 us (0.47); the launches traced: 228 us -> 108 us
  waiting for transfers between devices: 154 us -> 0 us
  Pallas kernels: 0 us -> 97.6 us
  matrix products: 28 us -> 0.49 us
  between operations: 15.5 us -> 2.14 us
  other arithmetic: 10 us -> 0.67 us
  local copies, waits for them, and re-layouts: 14.7 us -> 7.13 us
  starting transfers between devices: 6.04 us -> 0 us
    all_gather x5 -> x0, waiting for transfers between devices: 150 us -> none  [the longest x1 49.7 us: on_device(): lax.all_gather(w_img, 'req', axis=1, tiled=True)]
    pallas_call x0 -> x1, Pallas kernels: none -> 97.6 us  [split_heads(): pl.pallas_call(kernel, out_shape=(jax.ShapeDtypeStruct((LATC, height, wid...]
    dot_general x9 -> x1, matrix products: 28 us -> 0.49 us  [split_heads(): features = jnp.dot(taps, stacked, preferred_element_type=F32).astype(BF16)]
    reduce_sum x8 -> x0, other arithmetic: 8.91 us -> none  [the longest x1 7.02 us: absorb_block(): jnp.sum(weights, axis=2)]
    ppermute x2 -> x0, starting transfers between devices: 5.84 us -> none  [the longest x1 3.4 us: with_halo(): lax.ppermute(lax.slice_in_dim(block, block.shape[dim] - width, None, axis...]
    all_gather x2 -> x0, local copies, waits for them, and re-layouts: 5.2 us -> none  [the longest x1 2.6 us: on_device(): piece_keys = lax.all_gather(keys_img, 'blk', axis=0, tiled=True)]
    slice x6 -> x0, local copies, waits for them, and re-layouts: 3.04 us -> none  [the longest x2 1.13 us: on_device(): queries = qkv[:, :head_cols].reshape(tok_rows, head_count, HD)]
    unnamed x5 -> x0, waiting for transfers between devices: 2.45 us -> none
  transfers between devices with their start and end apart: 7 -> 0, of which waited for: 6 -> 0; matrix products, arithmetic and copies ran while one was open for 20% -> 0% of each run, Pallas kernels for 0% -> 0%
where the time goes in v1:
time: 108 us
  Pallas kernels  97.6 us (90%)
  local copies, waits for them, and re-layouts  7.13 us (7%)
  between operations  2.14 us (2%)
    pallas_call x1, Pallas kernels, split_heads(): pl.pallas_call(kernel, out_shape=(jax.ShapeDtypeStruct((LATC, height, wid...  97.6 us
    unnamed x15, local copies, waits for them, and re-layouts  4.82 us

profile of v1, /device:TPU:16, one launch (start us, length us, event | category | flops | bytes accessed | tf_op | source)
XLA Modules:
  0.0 108.0 jit_solution(3549364992665971676)
XLA Ops:
  2.0 0.7 compare_bitcast_fusion
  2.7 0.1 broadcast_in_dim.26
  2.8 0.8 copy.22
  3.6 0.0 copy-start.3
  3.6 0.0 copy-start.4
  3.6 1.0 reshape.49
  4.6 0.0 copy-start
  4.6 0.0 copy-start.1
  4.7 0.0 copy-start.2
  4.7 0.1 copy.18
  4.8 1.3 %copy.17.wf_ref = bf16[1536,64]{1,0:T(8,128)(2,1)S(1)} copy(bf16[1536,64]{0,1:T(8,128)(2,1)} %param.18) | data formatting | bytes 393216 | tf_op args[6]
  6.1 1.1 %pad.4.xt_ref = bf16[256,1536]{1,0:T(8,128)(2,1)S(1)} pad(bf16[154,1536]{1,0:T(8,128)(2,1)} %bitcast.34, bf16[]{:T(256)} %constant.19.clone.1), padding=0_102x0_0 | pad | bytes 1259522 | tf_op jit(solution)/shard_map/jit(_pad)/pad | solution.py:498
  7.2 0.0 copy-done.3
  7.2 0.0 copy-done.4
  7.2 0.0 copy-done
  7.2 0.0 copy-done.1
  7.2 0.0 copy-done.2
  7.2 97.6 %split_heads.1 = (f32[16,8,128]{2,1,0:T(8,128)S(1)}, f32[16,8,128]{2,1,0:T(8,128)S(1)}, bf16[144,1024]{1,0:T(8,128)(2,1)S(1)}) custom-call(bf16[256,1536]{1,0:T(8,128)(2,1)S(1)} %bitcast.25, bf16[256,1536]{1,0:T(8,128)(2,1)S(1)} %pad.4.xt_ref, f32[7,1536]{1,0:T(8,128)S(1)} %bitcast.27, bf16[288,1536]{1,0:T(8,128)(2,1)S(1)} %bitcast.24, ...), custom_call_target="tpu_custom_call" | custom-call | tf_op jit(solution)/shard_map/split_heads/pallas_call | solution.py:502
  104.8 0.5 convolution_convert_fusion
  105.3 1.5 %copy.19 = bf16[1,512,8,128]{3,2,1,0:T(8,128)(2,1)} copy(bf16[1,512,8,128]{1,3,2,0:T(8,128)(2,1)S(1)} %bitcast.31) | data formatting | bytes 2097152
  106.8 0.6 copy.27
  107.4 0.6 copy.28
  (5 shorter events, 0.0 us)
Async XLA Ops:
  3.6 3.6 %copy-start.3 = (bf16[96,1536]{1,0:T(8,128)(2,1)S(1)}, bf16[96,1536]{1,0:T(8,128)(2,1)}, u32[]{:S(2)}) copy-start(bf16[96,1536]{1,0:T(8,128)(2,1)} %wo_ref.1) | copy-start | bytes 884740
  3.6 3.6 %copy-start.4 = (f32[1,16,8,128]{3,2,1,0:T(8,128)S(1)}, f32[1,16,8,128]{3,2,1,0:T(8,128)}, u32[]{:S(2)}) copy-start(f32[1,16,8,128]{3,2,1,0:T(8,128)} %param.22) | copy-start | bytes 196612
  4.6 2.5 %copy-start = (bf16[1536,288]{0,1:T(8,128)(2,1)S(1)}, bf16[1536,288]{0,1:T(8,128)(2,1)}, u32[]{:S(2)}) copy-start(bf16[1536,288]{0,1:T(8,128)(2,1)} %param.15) | copy-start | bytes 2654212
  4.6 2.5 %copy-start.1 = (bf16[1,256,1536]{2,1,0:T(8,128)(2,1)S(1)}, bf16[1,256,1536]{2,1,0:T(8,128)(2,1)}, u32[]{:S(2)}) copy-start(bf16[1,256,1536]{2,1,0:T(8,128)(2,1)} %param.12) | copy-start | bytes 2359300
  4.7 2.5 %copy-start.2 = (bf16[1536,192]{0,1:T(8,128)(2,1)S(1)}, bf16[1536,192]{0,1:T(8,128)(2,1)}, u32[]{:S(2)}) copy-start(bf16[1536,192]{0,1:T(8,128)(2,1)} %param.16) | copy-start | bytes 1769476

commit v2 on v1

--- a/solution.py
+++ b/solution.py
@@ -236,20 +236,22 @@
 
     pieces = []
     for j in range(6):
+        via = j % 2
         cid = 8 * (j // 2) + 2 * z + j % 2
         off = pl.multiple_of((cid % 3) * CHUNK, CHUNK)
         pieces.append(
-            (wi_ref.at[pl.ds(off, CHUNK)], WI.at[pl.ds(j * CHUNK, CHUNK)], cid // 3, wi_send.at[j], wi_recv.at[j], l_sem.at[j])
+            (wi_ref.at[pl.ds(off, CHUNK)], WI.at[pl.ds(j * CHUNK, CHUNK)], cid // 3, via, wi_send.at[j], wi_recv.at[j], l_sem.at[j])
         )
-    for j in range(2):
+    for j in range(4):
+        part = pl.ds((j % 2) * CHUNK, CHUNK)
         pieces.append(
-            (wt_ref, WT.at[pl.ds(j * group, group)], 4 * j + z, wt_send.at[j], wt_recv.at[j], l_sem.at[6 + j])
+            (wt_ref.at[part], WT.at[pl.ds(j * CHUNK, CHUNK)], 4 * (j // 2) + z, j % 2, wt_send.at[j], wt_recv.at[j], l_sem.at[6 + j])
         )
 
-    for src, slot, owner, ss, rs, ls in pieces:
+    for src, slot, owner, via, ss, rs, ls in pieces:
         @pl.when(owner == r)
         def _():
-            for n, dev in enumerate((nx, ny, nd, sib)):
+            for n, dev in enumerate((nx, ny, sib)):
                 rcopy(src, slot, ss.at[n], rs, req=dev).start()
             pltpu.make_async_copy(src, slot, ls).start()
 
@@ -274,33 +276,65 @@
     def _():
         down(z).start()
 
+    def take(step):
+        low, high = z - step, z + step
+
+        @pl.when(low >= 0)
+        def _():
+            rcopy(H.at[low], H.at[low], z_send.at[0, low], h_recv.at[low], blk=z).wait_recv()
+
+            @pl.when(z < NTILE - 1)
+            def _():
+                up(low).start()
+
+        @pl.when(high < NTILE)
+        def _():
+            rcopy(H.at[high], H.at[high], z_send.at[1, high], h_recv.at[high], blk=z).wait_recv()
+
+            @pl.when(z > 0)
+            def _():
+                down(high).start()
+
     BIAS[z] = bias_ref[...]
     for step in range(1, NTILE):
         rcopy(BIAS.at[z], BIAS.at[z], b_send.at[step], b_recv.at[NTILE - step], blk=lax.rem(z + step, NTILE)).start()
 
     pl.loop(0, TXT_PAD // 32)(lambda i: norm_rows(i, xt_ref, HT, 3, 4))
 
-    for src, slot, owner, ss, rs, ls in pieces:
+    for src, slot, owner, via, ss, rs, ls in pieces:
+        near, onward = ((nx, ny), (ny, nx))[via]
+
+        @pl.when(jnp.logical_or(owner == nx, owner == ny))
+        def _():
+            rcopy(src, slot, ss.at[0], rs, req=sib).wait_recv()
+            rcopy(slot, slot, ss.at[0], rs, req=sib).start()
+
+        @pl.when(owner == near)
+        def _():
+            rcopy(slot, slot, ss.at[1], rs, req=onward).start()
+
+    take(1)
+
+    for src, slot, owner, via, ss, rs, ls in pieces:
         @pl.when(owner == r)
         def _():
             pltpu.make_async_copy(src, slot, ls).wait()
 
-        @pl.when(owner != r)
+        @pl.when(owner == nd)
         def _():
             rcopy(src, slot, ss.at[0], rs, req=sib).wait_recv()
-
-        far = jnp.logical_and(owner // 2 != r // 2, owner % 2 == r % 2)
-
-        @pl.when(far)
-        def _():
             rcopy(slot, slot, ss.at[0], rs, req=sib).start()
+
+        @pl.when(owner % 2 != r % 2)
+        def _():
+            rcopy(src, slot, ss.at[0], rs, req=sib).wait_recv()
 
     def wo_rows(dev):
         return WO.at[pl.ds(pl.multiple_of(dev * CHUNK, CHUNK), CHUNK)]
 
     for n, (k, dev) in enumerate(((2, nx), (4, ny), (6, nd), (1, sib))):
         rcopy(wo_ref, wo_rows(r), wo_send.at[n], wo_recv.at[k], req=dev).start()
-    pltpu.make_async_copy(wo_ref, wo_rows(r), l_sem.at[8]).start()
+    pltpu.make_async_copy(wo_ref, wo_rows(r), l_sem.at[10]).start()
 
     kv = nt_dot(HT[...], WT[...]).astype(BF16)
     K[tokens:, :] = kv[:, :group]
@@ -316,24 +350,9 @@
     project(z)
     for step in range(1, NTILE):
         low, high = z - step, z + step
-
-        @pl.when(low >= 0)
-        def _():
-            rcopy(H.at[low], H.at[low], z_send.at[0, low], h_recv.at[low], blk=z).wait_recv()
-
-            @pl.when(z < NTILE - 1)
-            def _():
-                up(low).start()
-
-        @pl.when(high < NTILE)
-        def _():
-            rcopy(H.at[high], H.at[high], z_send.at[1, high], h_recv.at[high], blk=z).wait_recv()
-
-            @pl.when(z > 0)
-            def _():
-                down(high).start()
-
-        if step == 1:
+        if step > 1:
+            take(step)
+        if step == 2:
             for n, (k, dev) in enumerate(((2, nx), (4, ny), (6, nd))):
                 rows_of = wo_rows(dev)
                 rcopy(wo_ref, rows_of, wo_send.at[n], wo_recv.at[k], req=sib).wait_recv()
@@ -371,7 +390,7 @@
         rcopy(A.at[step], AT.at[z], a_send.at[step], a_recv.at[NTILE - step], blk=t).start()
     AT[z] = attend(z)
 
-    pltpu.make_async_copy(wo_ref, wo_rows(r), l_sem.at[8]).wait()
+    pltpu.make_async_copy(wo_ref, wo_rows(r), l_sem.at[10]).wait()
     rcopy(wo_ref, wo_rows(sib), wo_send.at[3], wo_recv.at[1], req=sib).wait_recv()
     for n, (k, dev) in enumerate(((3, nx), (5, ny), (7, nd))):
         rcopy(wo_ref, wo_rows(flip(dev, 1)), wo_send.at[4 + n], wo_recv.at[k], req=sib).wait_recv()
@@ -429,17 +448,21 @@
     def _():
         DEC[count + 1] = jnp.zeros((LATC, width), BF16)
 
-    for src, slot, owner, ss, rs, ls in pieces:
+    for src, slot, owner, via, ss, rs, ls in pieces:
+        near = (nx, ny)[via]
+
         @pl.when(owner == r)
         def _():
-            for n, dev in enumerate((nx, ny, nd, sib)):
-                rcopy(src, slot, ss.at[n], rs, req=dev).wait_send()
-
-        far = jnp.logical_and(owner // 2 != r // 2, owner % 2 == r % 2)
-
-        @pl.when(far)
+            for n in range(3):
+                rcopy(src, slot, ss.at[n], rs, req=sib).wait_send()
+
+        @pl.when(jnp.logical_and(owner != r, owner % 2 == r % 2))
         def _():
             rcopy(slot, slot, ss.at[0], rs, req=sib).wait_send()
+
+        @pl.when(owner == near)
+        def _():
+            rcopy(slot, slot, ss.at[1], rs, req=sib).wait_send()
 
     for n in range(7):
         rcopy(wo_ref, wo_rows(r), wo_send.at[n], wo_recv.at[1], req=sib).wait_send()
@@ -528,15 +551,15 @@
             dma((NTILE,)),
             dma((6, 4)),
             dma((6,)),
-            dma((2, 4)),
-            dma((2,)),
+            dma((4, 4)),
+            dma((4,)),
             dma((7,)),
             dma((8,)),
             dma((NTILE,)),
             dma((NTILE,)),
             dma((2,)),
             dma((2,)),
-            dma((9,)),
+            dma((11,)),
         ],
         compiler_params=pltpu.CompilerParams(
             collective_id=0, has_side_effects=True, vmem_limit_bytes=48 * 1024 * 1024

time: 108 us -> 97.9 us (0.906)
  Pallas kernels: 97.6 us -> 87.2 us
    pallas_call x1, Pallas kernels: 97.6 us -> 87.2 us  [split_heads(): pl.pallas_call(kernel, out_shape=(jax.ShapeDtypeStruct((LATC, height, wid...]
where the time goes in v2:
time: 97.9 us; the launch traced here: 97.6 us
  Pallas kernels  87.2 us (89%)
  local copies, waits for them, and re-layouts  7.13 us (7%)
  between operations  2.14 us (2%)
    pallas_call x1, Pallas kernels, split_heads(): pl.pallas_call(kernel, out_shape=(jax.ShapeDtypeStruct((LATC, height, wid...  87.2 us
    unnamed x15, local copies, waits for them, and re-layouts  4.82 us

profile of v2, /device:TPU:16, one launch (start us, length us, event | category | flops | bytes accessed | tf_op | source)
XLA Modules:
  0.0 97.6 jit_solution(12634866596785160753)
XLA Ops:
  2.0 0.7 compare_bitcast_fusion
  2.7 0.1 broadcast_in_dim.26
  2.8 0.8 copy.22
  3.6 0.0 copy-start.3
  3.6 0.0 copy-start.4
  3.6 1.0 %reshape.49 = bf16[512,16,9]{0,2,1:T(8,128)(2,1)S(1)} reshape(bf16[512,144]{0,1:T(8,128)(2,1)} %param.23) | data formatting | bytes 294912 | tf_op jit(solution)/shard_map/reshape | solution.py:572
  4.6 0.0 copy-start
  4.6 0.0 copy-start.1
  4.7 0.0 copy-start.2
  4.7 0.1 copy.18
  4.8 1.3 %copy.17.wf_ref = bf16[1536,64]{1,0:T(8,128)(2,1)S(1)} copy(bf16[1536,64]{0,1:T(8,128)(2,1)} %param.18) | data formatting | bytes 393216 | tf_op args[6]
  6.1 1.1 %pad.4.xt_ref = bf16[256,1536]{1,0:T(8,128)(2,1)S(1)} pad(bf16[154,1536]{1,0:T(8,128)(2,1)} %bitcast.34, bf16[]{:T(256)} %constant.19.clone.1), padding=0_102x0_0 | pad | bytes 1259522 | tf_op jit(solution)/shard_map/jit(_pad)/pad | solution.py:521
  7.2 0.0 copy-done.3
  7.2 0.0 copy-done.4
  7.2 0.0 copy-done
  7.2 0.0 copy-done.1
  7.2 0.0 copy-done.2
  7.2 87.2 %split_heads.1 = (f32[16,8,128]{2,1,0:T(8,128)S(1)}, f32[16,8,128]{2,1,0:T(8,128)S(1)}, bf16[144,1024]{1,0:T(8,128)(2,1)S(1)}) custom-call(bf16[256,1536]{1,0:T(8,128)(2,1)S(1)} %bitcast.25, bf16[256,1536]{1,0:T(8,128)(2,1)S(1)} %pad.4.xt_ref, f32[7,1536]{1,0:T(8,128)S(1)} %bitcast.27, bf16[288,1536]{1,0:T(8,128)(2,1)S(1)} %bitcast.24, ...), custom_call_target="tpu_custom_call" | custom-call | tf_op jit(solution)/shard_map/split_heads/pallas_call | solution.py:525
  94.4 0.5 convolution_convert_fusion
  94.9 1.5 %copy.19 = bf16[1,512,8,128]{3,2,1,0:T(8,128)(2,1)} copy(bf16[1,512,8,128]{1,3,2,0:T(8,128)(2,1)S(1)} %bitcast.31) | data formatting | bytes 2097152
  96.3 0.6 copy.27
  97.0 0.6 copy.28
  (5 shorter events, 0.0 us)
Async XLA Ops:
  3.6 3.6 %copy-start.3 = (bf16[96,1536]{1,0:T(8,128)(2,1)S(1)}, bf16[96,1536]{1,0:T(8,128)(2,1)}, u32[]{:S(2)}) copy-start(bf16[96,1536]{1,0:T(8,128)(2,1)} %wo_ref.1) | copy-start | bytes 884740
  3.6 3.6 %copy-start.4 = (f32[1,16,8,128]{3,2,1,0:T(8,128)S(1)}, f32[1,16,8,128]{3,2,1,0:T(8,128)}, u32[]{:S(2)}) copy-start(f32[1,16,8,128]{3,2,1,0:T(8,128)} %param.22) | copy-start | bytes 196612
  4.6 2.5 %copy-start = (bf16[1536,288]{0,1:T(8,128)(2,1)S(1)}, bf16[1536,288]{0,1:T(8,128)(2,1)}, u32[]{:S(2)}) copy-start(bf16[1536,288]{0,1:T(8,128)(2,1)} %param.15) | copy-start | bytes 2654212
  4.6 2.5 %copy-start.1 = (bf16[1,256,1536]{2,1,0:T(8,128)(2,1)S(1)}, bf16[1,256,1536]{2,1,0:T(8,128)(2,1)}, u32[]{:S(2)}) copy-start(bf16[1,256,1536]{2,1,0:T(8,128)(2,1)} %param.12) | copy-start | bytes 2359300
  4.7 2.5 %copy-start.2 = (bf16[1536,192]{0,1:T(8,128)(2,1)S(1)}, bf16[1536,192]{0,1:T(8,128)(2,1)}, u32[]{:S(2)}) copy-start(bf16[1536,192]{0,1:T(8,128)(2,1)} %param.16) | copy-start | bytes 1769476

commit v3 on v2

--- a/solution.py
+++ b/solution.py
@@ -204,7 +204,7 @@
 def kernel(
     x_ref, xt_ref, mod_ref, wi_ref, wt_ref, wo_ref, wf_ref, bias_ref, ss_ref, lat_ref,
     vel_ref, next_ref, stk_ref,
-    H, HT, WI, WT, WO, Q, K, V, BIAS, A, AT, FIN, DEC,
+    H, HT, WI, WT, WO, Q, K, V, BIAS, A, AT, FIN, DEC, STK,
     z_send, h_recv, b_send, b_recv, wi_send, wi_recv, wt_send, wt_recv,
     wo_send, wo_recv, a_send, a_recv, d_send, d_recv, l_sem,
 ):
@@ -257,7 +257,7 @@
 
     def norm_rows(i, src, dst, shift, scale):
         at = pl.ds(pl.multiple_of(i * 32, 32), 32)
-        dst[at, :] = (normed(src[at, :]) * (1.0 + mod_ref[scale : scale + 1, :]) + mod_ref[shift : shift + 1, :]).astype(BF16)
+        dst[at, :] = (normed(src[at, :]) * (1.0 + mod_ref[scale]) + mod_ref[shift]).astype(BF16)
 
     own = H.at[z]
     pl.loop(0, rows // 32)(lambda i: norm_rows(i, x_ref, own, 0, 1))
@@ -299,7 +299,11 @@
     for step in range(1, NTILE):
         rcopy(BIAS.at[z], BIAS.at[z], b_send.at[step], b_recv.at[NTILE - step], blk=lax.rem(z + step, NTILE)).start()
 
-    pl.loop(0, TXT_PAD // 32)(lambda i: norm_rows(i, xt_ref, HT, 3, 4))
+    whole = xt_ref.shape[0] // 32 * 32
+    pl.loop(0, whole // 32)(lambda i: norm_rows(i, xt_ref, HT, 3, 4))
+    rest = (normed(xt_ref[whole:, :]) * (1.0 + mod_ref[4]) + mod_ref[3]).astype(BF16)
+    filler = jnp.zeros((TXT_PAD - xt_ref.shape[0], rest.shape[1]), BF16)
+    HT[whole:, :] = jnp.concatenate([rest, filler], axis=0)
 
     for src, slot, owner, via, ss, rs, ls in pieces:
         near, onward = ((nx, ny), (ny, nx))[via]
@@ -403,8 +407,8 @@
         proj = jnp.dot(AT[0, at, :], WO[0:group, :], preferred_element_type=F32)
         for s in range(1, NTILE):
             proj += jnp.dot(AT[s, at, :], WO[s * group : (s + 1) * group, :], preferred_element_type=F32)
-        res = x_ref[at, :].astype(F32) + mod_ref[2:3, :] * proj
-        FIN[at, :] = (normed(res) * (1.0 + mod_ref[6:7, :]) + mod_ref[5:6, :]).astype(BF16)
+        res = x_ref[at, :].astype(F32) + mod_ref[2] * proj
+        FIN[at, :] = (normed(res) * (1.0 + mod_ref[6]) + mod_ref[5]).astype(BF16)
 
     pl.loop(0, rows // 64)(out_rows)
 
@@ -413,7 +417,7 @@
         == lax.broadcasted_iota(jnp.int32, (2 * rows, rows), 1)
     ).astype(F32).astype(BF16)
     twice = jnp.dot(dup, FIN[...], preferred_element_type=F32).astype(BF16)
-    tok = jnp.dot(twice, wf_ref[...], preferred_element_type=F32).T
+    tok = nt_dot(wf_ref[...], twice)
     even = lax.broadcasted_iota(jnp.int32, (LATC, 2 * rows), 1) % 2 == 0
     width = PATCH * GRIDW
     sig = ss_ref[0:1, :]
@@ -502,7 +506,13 @@
             if 0 <= y < count:
                 for b in range(3):
                     at = (3 * a + b) * LATC
-                    stk_ref[at : at + LATC, y * width : (y + 1) * width] = shifted[b].astype(BF16)
+                    STK[at : at + LATC, y * width : (y + 1) * width] = shifted[b].astype(BF16)
+
+    taps = 9 * LATC
+    row = lax.broadcasted_iota(jnp.int32, (taps, taps), 0)
+    col = lax.broadcasted_iota(jnp.int32, (taps, taps), 1)
+    order = (row == (col % LATC) * 9 + col // LATC).astype(F32).astype(BF16)
+    stk_ref[...] = jnp.dot(order, STK[...], preferred_element_type=F32).astype(BF16)
 
 
 def split_heads(
@@ -518,7 +528,6 @@
     step_index = timestep[0]
     sigma_step = sigma_of(step_index + 1, NSTEPS) - sigma_of(step_index, NSTEPS)
     height, width = latent.shape[2], latent.shape[3]
-    xt = jnp.pad(x_txt[0], ((0, TXT_PAD - x_txt.shape[1]), (0, 0)))
     vmem = pl.BlockSpec(memory_space=pltpu.VMEM)
     hbm = pl.BlockSpec(memory_space=pl.ANY)
     dma = pltpu.SemaphoreType.DMA
@@ -545,6 +554,7 @@
             pltpu.VMEM((NTILE, rows, group), BF16),
             pltpu.VMEM((rows, model), BF16),
             pltpu.VMEM((height + 2, LATC, width), BF16),
+            pltpu.VMEM((9 * LATC, height * width), BF16),
             dma((2, NTILE)),
             dma((NTILE,)),
             dma((NTILE,)),
@@ -566,11 +576,10 @@
         ),
         name="split_heads",
     )(
-        x_img[0], xt, modulation[0], w_img.T, w_txt.T, w_out, w_final, bias,
+        x_img[0], x_txt[0], modulation.transpose(1, 0, 2), w_img.T, w_txt.T, w_out, w_final.T, bias,
         jnp.full((8, width), sigma_step, F32), latent[0],
     )
-    taps = conv_w.reshape(-1, LATC, 9).transpose(0, 2, 1).reshape(-1, 9 * LATC)
-    features = jnp.dot(taps, stacked, preferred_element_type=F32).astype(BF16)
+    features = jnp.dot(conv_w, stacked, preferred_element_type=F32).astype(BF16)
     return velocity[None], latent_next[None], features.reshape(1, -1, height, width)
 
 

time: 97.9 us -> 102 us (1.042)
  local copies, waits for them, and re-layouts: 7.13 us -> 10.7 us
    unnamed x15 -> x21, local copies, waits for them, and re-layouts: 4.82 us -> 10.6 us
    pad x1 -> x0, local copies, waits for them, and re-layouts: 1.09 us -> none  [split_heads(): xt = jnp.pad(x_txt[0], ((0, TXT_PAD - x_txt.shape[1]), (0, 0)))]
    reshape x1 -> x0, local copies, waits for them, and re-layouts: 1.03 us -> none  [split_heads(): taps = conv_w.reshape(-1, LATC, 9).transpose(0, 2, 1).reshape(-1, 9 * LATC)]
where the time goes in v3:
time: 102 us; the launch traced here: 101 us
  Pallas kernels  87.2 us (85%)
  local copies, waits for them, and re-layouts  10.7 us (10%)
  between operations  2.12 us (2%)
    pallas_call x1, Pallas kernels, split_heads(): pl.pallas_call(kernel, out_shape=(jax.ShapeDtypeStruct((LATC, height, wid...  87.2 us
    unnamed x21, local copies, waits for them, and re-layouts  10.6 us

profile of v3, /device:TPU:16, one launch (start us, length us, event | category | flops | bytes accessed | tf_op | source)
XLA Modules:
  0.0 101.2 jit_solution(9560017962257225844)
XLA Ops:
  0.6 0.0 copy-start
  2.1 0.7 compare_bitcast_fusion
  2.7 0.1 broadcast_in_dim.26
  2.9 0.0 copy-start.1
  2.9 1.2 %copy-done.1 = bf16[1536,288]{0,1:T(8,128)(2,1)S(1)} copy-done((bf16[1536,288]{0,1:T(8,128)(2,1)S(1)}, bf16[1536,288]{0,1:T(8,128)(2,1)}, u32[]{:S(2)}) %copy-start.1) | copy-done | bytes 884760
  4.0 0.0 copy-start.2
  4.0 1.1 %copy-done.2 = bf16[1,256,1536]{2,1,0:T(8,128)(2,1)S(1)} copy-done((bf16[1,256,1536]{2,1,0:T(8,128)(2,1)S(1)}, bf16[1,256,1536]{2,1,0:T(8,128)(2,1)}, u32[]{:S(2)}) %copy-start.2) | copy-done | bytes 786456
  5.2 0.0 copy-start.3
  5.2 1.1 %copy-done.3 = bf16[1536,192]{0,1:T(8,128)(2,1)S(1)} copy-done((bf16[1536,192]{0,1:T(8,128)(2,1)S(1)}, bf16[1536,192]{0,1:T(8,128)(2,1)}, u32[]{:S(2)}) %copy-start.3) | copy-done | bytes 589848
  6.2 0.0 copy-start.4
  6.2 1.0 %copy-done.4 = bf16[1,154,1536]{2,1,0:T(8,128)(2,1)S(1)} copy-done((bf16[1,154,1536]{2,1,0:T(8,128)(2,1)S(1)}, bf16[1,154,1536]{2,1,0:T(8,128)(2,1)}, u32[]{:S(2)}) %copy-start.4) | copy-done | bytes 473112
  7.3 0.0 copy-start.5
  7.3 1.0 copy-done.5
  8.2 0.0 copy-start.6
  8.2 0.9 copy-done.6
  9.1 0.0 copy-start.7
  9.1 0.8 copy-done.7
  10.0 0.0 copy-start.8
  10.0 0.8 copy-done.8
  10.8 87.2 %split_heads.1 = (f32[16,8,128]{2,1,0:T(8,128)S(1)}, f32[16,8,128]{2,1,0:T(8,128)S(1)}, bf16[144,1024]{1,0:T(8,128)(2,1)S(1)}) custom-call(bf16[256,1536]{1,0:T(8,128)(2,1)S(1)} %bitcast.20, bf16[154,1536]{1,0:T(8,128)(2,1)S(1)} %bitcast.22, f32[7,1,1536]{2,1,0:T(1,128)S(1)} %bitcast.27, bf16[288,1536]{1,0:T(8,128)(2,1)S(1)} %bitcast.19, ...), custom_call_target="tpu_custom_call" | custom-call | tf_op jit(solution)/shard_map/split_heads/pallas_call | solution.py:534
  98.0 0.0 copy-done
  98.0 0.5 convolution_convert_fusion
  98.5 1.5 %copy.15 = bf16[1,512,8,128]{3,2,1,0:T(8,128)(2,1)} copy(bf16[1,512,8,128]{1,3,2,0:T(8,128)(2,1)S(1)} %bitcast.28) | data formatting | bytes 2097152
  100.0 0.6 copy.20
  100.6 0.6 copy.21
  (5 shorter events, 0.0 us)
Async XLA Ops:
  0.6 97.4 %copy-start = (bf16[512,144]{0,1:T(8,128)(2,1)S(1)}, bf16[512,144]{0,1:T(8,128)(2,1)}, u32[]{:S(2)}) copy-start(bf16[512,144]{0,1:T(8,128)(2,1)} %param.23) | copy-start | bytes 442372
  2.9 1.2 %copy-start.1 = (bf16[1536,288]{0,1:T(8,128)(2,1)S(1)}, bf16[1536,288]{0,1:T(8,128)(2,1)}, u32[]{:S(2)}) copy-start(bf16[1536,288]{0,1:T(8,128)(2,1)} %param.15) | copy-start | bytes 2654212
  4.0 1.1 %copy-start.2 = (bf16[1,256,1536]{2,1,0:T(8,128)(2,1)S(1)}, bf16[1,256,1536]{2,1,0:T(8,128)(2,1)}, u32[]{:S(2)}) copy-start(bf16[1,256,1536]{2,1,0:T(8,128)(2,1)} %param.12) | copy-start | bytes 2359300
  5.2 1.1 %copy-start.3 = (bf16[1536,192]{0,1:T(8,128)(2,1)S(1)}, bf16[1536,192]{0,1:T(8,128)(2,1)}, u32[]{:S(2)}) copy-start(bf16[1536,192]{0,1:T(8,128)(2,1)} %param.16) | copy-start | bytes 1769476
  6.2 1.0 %copy-start.4 = (bf16[1,154,1536]{2,1,0:T(8,128)(2,1)S(1)}, bf16[1,154,1536]{2,1,0:T(8,128)(2,1)}, u32[]{:S(2)}) copy-start(bf16[1,154,1536]{2,1,0:T(8,128)(2,1)} %param.13) | copy-start | bytes 1419268
  7.3 1.0 copy-start.5
  8.2 0.9 copy-start.6
  9.1 0.8 copy-start.7
  10.0 0.8 copy-start.8

commit v4 on v3

--- a/solution.py
+++ b/solution.py
@@ -232,6 +232,13 @@
         pl.semaphore_signal(
             barrier, inc=1, device_id={"blk": lax.rem(z + step, NTILE)}, device_id_type=MESH
         )
+    def norm_rows(i, src, dst, shift, scale):
+        at = pl.ds(pl.multiple_of(i * 32, 32), 32)
+        dst[at, :] = (normed(src[at, :]) * (1.0 + mod_ref[scale]) + mod_ref[shift]).astype(BF16)
+
+    own = H.at[z]
+    pl.loop(0, rows // 32)(lambda i: norm_rows(i, x_ref, own, 0, 1))
+
     pl.semaphore_wait(barrier, NREQ - 1 + NTILE - 1)
 
     pieces = []
@@ -248,33 +255,26 @@
             (wt_ref.at[part], WT.at[pl.ds(j * CHUNK, CHUNK)], 4 * (j // 2) + z, j % 2, wt_send.at[j], wt_recv.at[j], l_sem.at[6 + j])
         )
 
+    def up(t):
+        return rcopy(H.at[t], H.at[t], z_send.at[0, t], h_recv.at[t], blk=z + 1)
+
+    def down(t):
+        return rcopy(H.at[t], H.at[t], z_send.at[1, t], h_recv.at[t], blk=z - 1)
+
+    @pl.when(z < NTILE - 1)
+    def _():
+        up(z).start()
+
+    @pl.when(z > 0)
+    def _():
+        down(z).start()
+
     for src, slot, owner, via, ss, rs, ls in pieces:
         @pl.when(owner == r)
         def _():
             for n, dev in enumerate((nx, ny, sib)):
                 rcopy(src, slot, ss.at[n], rs, req=dev).start()
             pltpu.make_async_copy(src, slot, ls).start()
-
-    def norm_rows(i, src, dst, shift, scale):
-        at = pl.ds(pl.multiple_of(i * 32, 32), 32)
-        dst[at, :] = (normed(src[at, :]) * (1.0 + mod_ref[scale]) + mod_ref[shift]).astype(BF16)
-
-    own = H.at[z]
-    pl.loop(0, rows // 32)(lambda i: norm_rows(i, x_ref, own, 0, 1))
-
-    def up(t):
-        return rcopy(H.at[t], H.at[t], z_send.at[0, t], h_recv.at[t], blk=z + 1)
-
-    def down(t):
-        return rcopy(H.at[t], H.at[t], z_send.at[1, t], h_recv.at[t], blk=z - 1)
-
-    @pl.when(z < NTILE - 1)
-    def _():
-        up(z).start()
-
-    @pl.when(z > 0)
-    def _():
-        down(z).start()
 
     def take(step):
         low, high = z - step, z + step
@@ -572,7 +572,7 @@
             dma((11,)),
         ],
         compiler_params=pltpu.CompilerParams(
-            collective_id=0, has_side_effects=True, vmem_limit_bytes=48 * 1024 * 1024
+            collective_id=0, has_side_effects=True, vmem_limit_bytes=60 * 1024 * 1024
         ),
         name="split_heads",
     )(

time: 102 us -> 95.4 us (0.935)
  local copies, waits for them, and re-layouts: 10.7 us -> 4.05 us
    unnamed x21 -> x9, local copies, waits for them, and re-layouts: 10.6 us -> 2.74 us
where the time goes in v4:
time: 95.4 us; the launch traced here: 95.2 us
  Pallas kernels  87 us (91%)
  local copies, waits for them, and re-layouts  4.05 us (4%)
  between operations  2.11 us (2%)
  matrix products  1.44 us (2%)
    pallas_call x1, Pallas kernels, split_heads(): pl.pallas_call(kernel, out_shape=(jax.ShapeDtypeStruct((LATC, height, wid...  87 us
    unnamed x9, local copies, waits for them, and re-layouts  2.74 us

profile of v4, /device:TPU:16, one launch (start us, length us, event | category | flops | bytes accessed | tf_op | source)
XLA Modules:
  0.0 95.2 jit_solution(2819875035132937185)
XLA Ops:
  0.6 0.0 copy-start
  2.1 0.7 compare_bitcast_fusion
  2.7 0.1 broadcast_in_dim.26
  2.8 0.6 broadcast_in_dim.30.ss_ref
  3.4 0.6 broadcast_in_dim.29.bias_ref
  4.1 87.0 %split_heads.1 = (f32[16,8,128]{2,1,0:T(8,128)}, f32[16,8,128]{2,1,0:T(8,128)}, bf16[144,1024]{1,0:T(8,128)(2,1)}) custom-call(bf16[256,1536]{1,0:T(8,128)(2,1)} %bitcast.21, bf16[154,1536]{1,0:T(8,128)(2,1)} %bitcast.23, f32[7,1,1536]{2,1,0:T(1,128)} %bitcast.28, bf16[288,1536]{1,0:T(8,128)(2,1)} %bitcast.20, bf16[192,1536]{1,0:T(8,128)(2,1)} %bitcast.22, ...), custom_call_target="tpu_custom_call" | custom-call | tf_op jit(solution)/shard_map/split_heads/pallas_call | solution.py:534
  91.0 0.0 copy-done
  91.0 1.4 %convolution_convert_fusion = bf16[1024,512]{1,0:T(8,128)(2,1)S(1)} fusion(bf16[144,1024]{1,0:T(8,128)(2,1)} %get-tuple-element.8, bf16[512,144]{0,1:T(8,128)(2,1)S(1)} %copy-done), kind=kOutput, calls=%fused_computation | convolution fusion | flops 151519232 | bytes 1490944 | tf_op jit(solution)/shard_map/dot_general | solution.py:582
  92.5 0.0 copy-start.2
  92.5 0.0 copy-start.1
  92.5 1.5 %copy.15 = bf16[1,512,8,128]{3,2,1,0:T(8,128)(2,1)} copy(bf16[1,512,8,128]{1,3,2,0:T(8,128)(2,1)S(1)} %bitcast.19) | data formatting | bytes 2097152
  94.0 0.0 copy-done.2
  94.0 0.6 copy.20
  94.6 0.0 copy-done.1
  94.6 0.6 copy.21
  (3 shorter events, 0.0 us)
Async XLA Ops:
  0.6 90.4 %copy-start = (bf16[512,144]{0,1:T(8,128)(2,1)S(1)}, bf16[512,144]{0,1:T(8,128)(2,1)}, u32[]{:S(2)}) copy-start(bf16[512,144]{0,1:T(8,128)(2,1)} %param.23) | copy-start | bytes 442372
  92.5 1.5 %copy-start.2 = (f32[16,8,128]{2,1,0:T(8,128)S(1)}, f32[16,8,128]{2,1,0:T(8,128)}, u32[]{:S(2)}) copy-start(f32[16,8,128]{2,1,0:T(8,128)} %get-tuple-element.6) | copy-start | bytes 196612
  92.5 2.1 %copy-start.1 = (f32[16,8,128]{2,1,0:T(8,128)S(1)}, f32[16,8,128]{2,1,0:T(8,128)}, u32[]{:S(2)}) copy-start(f32[16,8,128]{2,1,0:T(8,128)} %get-tuple-element.7) | copy-start | bytes 196612
